TPU v7x, 32 devices: a whole 2x2x4 slice. The times are simulated.
32 devices in a mesh: fsdp: 4 (over z), ctx: 4 (over x, core), tp: 2 (over y).
Axes of the slice: x: 2, y: 2, z: 4, core: 2. Of those that a mesh axis runs over, the one named last changes fastest.
Arguments:
- tokens: bfloat16 [8192, 1024], P(('fsdp', 'ctx'), 'tp'), may hold values from -6 to 6
- cotangent: bfloat16 [8192, 1024], P(('fsdp', 'ctx'), 'tp'), may hold values from -6 to 6
- slot_of: int32 [8192], replicated, may hold values from 0 to 8191, as said below
- lengths: int32 [4, 3], P('fsdp'), may hold values from 0 to 2048, as said below
- w_query: bfloat16 [1024, 1024], P(('fsdp', 'ctx'), 'tp'), may hold values from -0.1875 to 0.1875
- key_weight: bfloat16 [1024, 512], P(('fsdp', 'ctx'), 'tp'), may hold values from -0.1875 to 0.1875
- value_weight: bfloat16 [1024, 512], P(('fsdp', 'ctx'), 'tp'), may hold values from -0.1875 to 0.1875
- w_out: bfloat16 [1024, 1024], P('tp', ('fsdp', 'ctx')), may hold values from -3 to 3
- w_gate: bfloat16 [1024, 4608], P(('fsdp', 'ctx'), 'tp'), may hold values from -0.1875 to 0.1875
- w_up: bfloat16 [1024, 4608], P(('fsdp', 'ctx'), 'tp'), may hold values from -0.1875 to 0.1875
- w_down: bfloat16 [4608, 1024], P('tp', ('fsdp', 'ctx')), may hold values from -0.09375 to 0.09375
- gain_attn: float32 [1024], replicated, may hold values from 0.25 to 1.75
- gain_ffn: float32 [1024], replicated, may hold values from 0.25 to 1.75
- gain_query: float32 [64], replicated, may hold values from 0.25 to 1.75
- gain_key: float32 [64], replicated, may hold values from 0.25 to 1.75
Outputs:
- output: bfloat16 [8192, 1024], P(('fsdp', 'ctx'), 'tp')
- grad_tokens: bfloat16 [8192, 1024], P(('fsdp', 'ctx'), 'tp')
- grad_w_query: float32 [1024, 1024], P(('fsdp', 'ctx'), 'tp')
- grad_w_key: float32 [1024, 512], P(('fsdp', 'ctx'), 'tp')
- grad_w_value: float32 [1024, 512], P(('fsdp', 'ctx'), 'tp')
- grad_w_out: float32 [1024, 1024], P('tp', ('fsdp', 'ctx'))
- grad_w_gate: float32 [1024, 4608], P(('fsdp', 'ctx'), 'tp')
- grad_w_up: float32 [1024, 4608], P(('fsdp', 'ctx'), 'tp')
- grad_w_down: float32 [4608, 1024], P('tp', ('fsdp', 'ctx'))
- grad_gain_attn: float32 [1024], replicated
- grad_gain_ffn: float32 [1024], replicated
- grad_gain_query: float32 [64], replicated
- grad_gain_key: float32 [64], replicated
- rms_stats: float32 [3], replicated
Inputs may be any that keep to these rules, and one draw needn't show every extreme that they name: slot_of is a permutation of the 8192 slots; the tokens of each index of fsdp+ctx go in equal shares to the slots held by every index of fsdp+ctx (each index holds one piece of 2048 / 4 slots of its row). Each row's lengths sum to 2048; its nonzero lengths come first and are at least 512; a row holds one to three sequences, and the first row holds one.
All inputs are finite; a program needn't handle non-finite values.
Results may differ from a plain program's by a relative error of at most 0.024.
Values may be sent and summed in bfloat16 or wider, within the bound.
A program may use at most 256 MiB of HBM per device.

v0:
```python
import functools

import jax
import jax.numpy as jnp
import numpy as np
from jax import lax
from jax.experimental import pallas as pl
from jax.experimental.pallas import tpu as pltpu
from jax.sharding import PartitionSpec as P

MODEL_WIDTH = 1024
QUERY_HEADS = 16
KEY_VALUE_HEADS = 8
HEAD_SIZE = 64

EPSILON = 1e-05
ROPE_THETA = 1000000.0
NEG_FILL = -1e30
BF = jnp.bfloat16
F32 = jnp.float32


class Grid:
    def __init__(self):
        self.n = lax.axis_size("fsdp")
        self.ctx = lax.axis_size("ctx")
        self.tp = lax.axis_size("tp")
        self.z = lax.axis_index("fsdp")
        self.c = lax.axis_index("ctx")
        self.t = lax.axis_index("tp")


def shape(s, t):
    return jax.ShapeDtypeStruct(s, t)


ANYWHERE = pl.BlockSpec(memory_space=pl.ANY)


def dot(a, b, ca, cb, precision=None):
    return lax.dot_general(
        a, b, (((ca,), (cb,)), ((), ())), preferred_element_type=F32, precision=precision
    )


def lanes(shape):
    return lax.broadcasted_iota(jnp.int32, shape, 1)


def half_mean(v):
    low = lanes(v.shape) < HEAD_SIZE
    first = jnp.sum(jnp.where(low, v, 0.0), axis=1, keepdims=True)
    second = jnp.sum(jnp.where(low, 0.0, v), axis=1, keepdims=True)
    return jnp.where(low, first, second) * (1.0 / HEAD_SIZE)


def half_swap(v):
    quarter = HEAD_SIZE // 2
    left = pltpu.roll(v, 128 - quarter, 1)
    right = pltpu.roll(v, quarter, 1)
    return jnp.where(lanes(v.shape) % HEAD_SIZE < quarter, left, right)


def row_scale(v):
    return lax.rsqrt(jnp.mean(v * v, axis=1, keepdims=True) + EPSILON)


def norm_back(dn, v, gain):
    scale = row_scale(v)
    unit = v * scale
    scaled = dn * gain
    grad = scale * (scaled - unit * jnp.mean(scaled * unit, axis=1, keepdims=True))
    return grad, jnp.sum(dn * unit, axis=0, keepdims=True)


def qk_forward(raw, gain, cosines, sines, is_value):
    normed = raw * lax.rsqrt(half_mean(raw * raw) + EPSILON) * gain
    turned = normed * cosines + half_swap(normed) * sines
    return jnp.where(is_value, raw, turned)


def qk_backward(grad, raw, gain, cosines, sines, is_value):
    straight = grad * cosines - half_swap(grad) * sines
    scale = lax.rsqrt(half_mean(raw * raw) + EPSILON)
    unit = raw * scale
    scaled = straight * gain
    back = scale * (scaled - unit * half_mean(scaled * unit))
    gain_grad = jnp.sum(straight * unit, axis=0, keepdims=True)
    return jnp.where(is_value, grad, back), gain_grad


def two_heads(v):
    low = lanes(v.shape) < HEAD_SIZE
    zero = jnp.zeros_like(v)
    return jnp.concatenate([jnp.where(low, v, zero), jnp.where(low, zero, v)], axis=0)


def one_row(v):
    rows = v.shape[0] // 2
    return jnp.where(lanes((rows, v.shape[1])) < HEAD_SIZE, v[:rows], v[rows:])


def twice(v, which):
    half = v[:, which * HEAD_SIZE : (which + 1) * HEAD_SIZE]
    return jnp.concatenate([half, half], axis=1)


def both_halves(v):
    return v + jnp.concatenate([v[:, HEAD_SIZE:], v[:, :HEAD_SIZE]], axis=1)


def over_key_heads(n_heads, values_from, body):
    if n_heads % 2:
        for g in range(n_heads):
            body([(g, (g // 2, g % 2), ((values_from + g) // 2, (values_from + g) % 2))])
        return

    def step(i, carry):
        body([(2 * i + e, (i, e), (values_from // 2 + i, e)) for e in range(2)])
        return carry

    lax.fori_loop(0, n_heads // 2, step, 0)


def lane_block(i):
    return block_rows(i, 128)


def segment_start(lengths, slots):
    end = lengths[0, 0]
    start = jnp.where(slots >= end, end, 0)
    for i in range(1, lengths.shape[1] - 1):
        end = end + lengths[0, i]
        start = jnp.where(slots >= end, end, start)
    return start


def sublanes(shape):
    return lax.broadcasted_iota(jnp.int32, shape, 0)


def count(mask, axis):
    return jnp.sum(mask.astype(F32), axis=axis, keepdims=True).astype(jnp.int32)


def routing(place, slots, rows, share):
    lines = rows // 128
    groups = slots.shape[0] // lines
    square = (rows, rows)

    def line(s):
        return jnp.concatenate([slots[pl.ds(s * lines + i, 1), :] for i in range(lines)], axis=1)

    row = line(place.me)
    column = jnp.broadcast_to(row.astype(F32), (128, rows)).T[:, :1].astype(jnp.int32)
    base = row // rows * rows
    rank = count((column < row) & (column >= base), 0)
    sent_row = row // rows * share + rank
    base = column // rows * rows
    rank = count((row < column) & (row >= base), 1)
    sent_column = column // rows * share + rank
    low = 32
    high = rows // low
    table = jnp.zeros((high, low), F32)
    for s in range(groups):
        r = line(s)
        left = (r // low - place.me * high) == sublanes((high, rows))
        right = r % low == sublanes((low, rows))
        table = table + dot(left.astype(BF), right.astype(BF), 1, 1) * float(s)
    spread = (lanes((low, rows)) % low == sublanes((low, rows))).astype(F32)
    pick = lanes((high, rows)) // low == sublanes((high, rows))
    from_row = jnp.sum(jnp.where(pick, dot(table, spread, 1, 0), 0.0), axis=0, keepdims=True)
    spread = (sublanes((rows, low)) % low == lanes((rows, low))).astype(F32)
    pick = sublanes((rows, high)) // low == lanes((rows, high))
    from_column = jnp.sum(jnp.where(pick, dot(spread, table, 1, 1), 0.0), axis=1, keepdims=True)
    from_row, from_column = from_row.astype(jnp.int32), from_column.astype(jnp.int32)
    same = from_row == from_column
    got_column = from_column * share + count(same & (lanes(square) < sublanes(square)), 1)
    got_row = from_row * share + count(same & (sublanes(square) < lanes(square)), 0)
    return sent_row, sent_column, got_row, got_column


class Place:
    def __init__(self, n, ctx, tp):
        self.n, self.ctx, self.tp = n, ctx, tp
        self.z = lax.axis_index("fsdp")
        self.c = lax.axis_index("ctx")
        self.t = lax.axis_index("tp")
        self.me = self.z * ctx + self.c

    def at(self, z=None, c=None, t=None):
        return (
            self.z if z is None else z,
            self.c if c is None else c,
            self.t if t is None else t,
        )

    def peer(self, j):
        p = lax.rem(self.me + j, self.n * self.ctx)
        return self.at(p // self.ctx, lax.rem(p, self.ctx))

    def up(self, j):
        return self.at(z=lax.rem(self.z + j, self.n))

    def flip(self, bit):
        if bit == 1:
            return self.c + 1 - 2 * lax.rem(self.c, 2)
        return lax.rem(self.c + 2, 4)

    def side(self, j):
        return self.at(t=lax.rem(self.t + j, self.tp))

    def owner(self, k, c):
        return lax.rem(self.z - k + self.n, self.n) * self.ctx + c

    def greet(self):
        barrier = pltpu.get_barrier_semaphore()
        group = self.n * self.ctx
        for j in range(1, group):
            pl.semaphore_signal(barrier, inc=1, device_id=self.peer(j), device_id_type=MESH)
        for j in range(1, self.tp):
            pl.semaphore_signal(barrier, inc=1, device_id=self.side(j), device_id_type=MESH)
        pl.semaphore_wait(barrier, group + self.tp - 2)


MESH = pl.DeviceIdType.MESH


def remote(src, dst, send, recv, device):
    return pltpu.make_async_remote_copy(
        src_ref=src, dst_ref=dst, send_sem=send, recv_sem=recv, device_id=device, device_id_type=MESH
    )


def block_rows(index, size):
    return pl.ds(pl.multiple_of(index * size, size), size)


class Gather:
    def __init__(self, place, whole, columns, number, sems, chip_first=False):
        z_send, z_recv, x_send, x_recv, c_send, c_recv = sems
        h = whole.shape[0] // (place.n * place.ctx)
        n = place.n
        self.n, self.chip_first = n, chip_first
        view = lambda index: whole.at[block_rows(index, h), columns]
        here, there = place.c, place.flip(2)

        def ring(lane, row):
            return [
                remote(
                    view(place.owner(k - 1, lane)),
                    view(place.owner(k - 1, lane)),
                    z_send.at[row, k],
                    z_recv.at[row, k],
                    place.up(1),
                )
                for k in range(1, n)
            ]

        self.rings = [ring(here, number)] + ([ring(there, number + 1)] if chip_first else [])
        self.chip = [
            remote(
                view(place.owner(k, here)),
                view(place.owner(k, here)),
                x_send.at[number, k],
                x_recv.at[number, k],
                place.at(c=there),
            )
            for k in range(1 if chip_first else n)
        ]
        self.core = [
            remote(
                view(place.owner(i % n, here if i < n else there)),
                view(place.owner(i % n, here if i < n else there)),
                c_send.at[number, i],
                c_recv.at[number, i],
                place.at(c=place.flip(1)),
            )
            for i in range(2 * n)
        ]

    def begin(self):
        if self.n > 1:
            self.rings[0][0].start()
        self.core[0].start()

    def begin_other(self):
        if self.n > 1:
            self.rings[1][0].start()

    def advance(self, k):
        if k >= self.n:
            return
        for r, ring in enumerate(self.rings):
            ring[k - 1].wait_recv()
            if k + 1 < self.n:
                ring[k].start()
            self.core[r * self.n + k].start()

    def to_chip(self, k):
        if k < len(self.chip):
            self.chip[k].start()

    def from_chip(self, k):
        if k < len(self.chip):
            self.chip[k].wait_recv()
            self.core[self.n + k].start()

    def finish(self):
        for copy in self.core:
            copy.wait_recv()

    def drain(self):
        for copy in sum(self.rings, []) + self.chip + self.core:
            copy.wait_send()


def forward_kernel(
    n, ctx, tp, q_width, kv_width, tile,
    lengths, tokens, cotangent, slots, gain, head_gain, gain_ffn, frequency,
    w_query, w_key, w_value, w_out, w_gate, w_up, w_down,
    sums, squares, ffn_out, dmid, dgain, take_back, send_back, cosines, sines,
    x, dy, qb_out, kv, heads_out, mid_own, w_attn, normed_two, hidden, d_gate, d_up,
    sent_x, sent_y, got_x, got_y, own_x, own_y, x_land, y_land, pick, qb, heads, mid, nb,
    w, w_ffn, kv_all, part, land, acc, total, bias, ffn_acc, dn_acc, acts,
    route_send, route_recv, tp_send, tp_recv, kv_send, kv_recv, out_sem, act_sem, *gather_sems
):
    place = Place(n, ctx, tp)
    group = n * ctx
    rows = got_x.shape[0]
    share = rows // group
    feat = got_x.shape[1]
    width = x_land.shape[1]
    piece = rows
    attn = Gather(place, w, pl.ds(0, w.shape[1]), 0, gather_sems)
    tiles = w_ffn.shape[1] // (3 * tile)
    last = max(1, tiles // 9)
    cuts = [(tiles - last) * i // 3 for i in range(3)] + [tiles - last, tiles]
    first, second, third, tail = (
        Gather(
            place,
            w_ffn,
            pl.ds(cuts[i] * 3 * tile, (cuts[i + 1] - cuts[i]) * 3 * tile),
            1 + i,
            gather_sems,
            chip_first=i == 3,
        )
        for i in range(4)
    )
    groups = [first, second, third]
    stores = []

    def store(src, dst):
        copy = pltpu.make_async_copy(src, dst, out_sem.at[len(stores)])
        copy.start()
        stores.append(copy)

    def route(number, src, dst):
        return [
            remote(
                src.at[block_rows(lax.rem(place.me + j, group), share), :],
                dst.at[block_rows(place.me, share), :],
                route_send.at[number, j],
                route_recv.at[number, j],
                place.peer(j),
            )
            for j in range(1, group)
        ]

    def widen(number, src, dst):
        return [
            remote(
                src,
                dst.at[:, block_rows(place.t, feat)],
                tp_send.at[number, j],
                tp_recv.at[number, j],
                place.side(j),
            )
            for j in range(1, tp)
        ]

    def own_block(src, dst):
        at = block_rows(place.me, share)
        dst[at, :] = src[at, :]

    route_x, route_y = route(0, sent_x, got_x), route(1, sent_y, got_y)
    wide_x, wide_y = widen(0, own_x, x_land), widen(1, own_y, y_land)
    shard_rows = w_query.shape[0]
    own_shard = block_rows(place.me, shard_rows)
    column = 0
    for part_w in (w_query, w_key, w_value):
        w[own_shard, column : column + part_w.shape[1]] = part_w[...]
        column += part_w.shape[1]
    w[own_shard, column:] = w_out[...]
    place.greet()
    attn.begin()
    attn.to_chip(0)
    sent_row, sent_column, got_row, got_column = routing(place, slots, rows, share)
    for i in range(tiles):
        used = min(tile, w_gate.shape[1] - i * tile)
        cols = slice(i * tile, i * tile + used)
        for m, value in enumerate((w_gate[:, cols], w_up[:, cols], w_down[:, cols])):
            if used < tile:
                value = jnp.concatenate(
                    [value, jnp.zeros((shard_rows, tile - used), BF)], axis=1
                )
            c = (3 * i + m) * tile
            w_ffn[own_shard, c : c + tile] = value
    square = (rows, rows)
    send_pick = (sublanes(square) == sent_row).astype(BF)
    sent_x[...] = dot(send_pick, tokens[...], 1, 0).astype(BF)
    for copy in route_x:
        copy.start()
    own_block(sent_x, got_x)
    attn.advance(1)
    attn.to_chip(1)
    sent_y[...] = dot(send_pick, cotangent[...], 1, 0).astype(BF)
    own_block(sent_y, got_y)
    pick[...] = (lanes(square) == got_column).astype(BF)
    take_back[...] = (sublanes(square) == got_row).astype(BF)
    send_back[...] = (lanes(square) == sent_column).astype(BF)
    slot = place.c * piece + sublanes((rows, 128))
    start_col = segment_start(lengths, slot)
    angle = (slot - start_col).astype(F32) * frequency[...]
    start_col = start_col[:, :1]
    cosines[...] = jnp.cos(angle)
    turned_lane = lanes((rows, 128)) % HEAD_SIZE < HEAD_SIZE // 2
    sines[...] = jnp.where(turned_lane, -1.0, 1.0) * jnp.sin(angle)
    attn.from_chip(0)
    attn.advance(2)
    attn.to_chip(2)
    first.begin()
    for copy in route_x:
        copy.wait_recv()
    own_x[...] = dot(pick[...], got_x[...], 1, 0).astype(BF)
    for copy in wide_x:
        copy.start()
    x_land[:, block_rows(place.t, feat)] = own_x[...]
    attn.from_chip(1)
    attn.advance(3)
    attn.to_chip(3)
    for copy in route_y:
        copy.start()
    second.begin()
    first.to_chip(0)
    attn.from_chip(2)
    attn.from_chip(3)
    second.to_chip(0)
    for copy in wide_x:
        copy.wait_recv()
    store(x_land, x)
    v = x_land[...].astype(F32)
    normed = (v * row_scale(v) * gain[...]).astype(BF)
    attn.finish()
    store(w, w_attn)

    own_rows = block_rows(place.c, piece)
    values_from = q_width + kv_width
    for b in list(range(q_width, q_width + 2 * kv_width, 128)) + list(range(0, q_width, 128)):
        if b == 0:
            later = start_keys(place, kv_all, own_rows, kv_send, kv_recv)
        block = dot(normed, w[:, b : b + 128], 1, 0)
        is_value = lanes(block.shape) + b >= values_from
        done = qk_forward(block, head_gain[:, b : b + 128], cosines[...], sines[...], is_value)
        if b < q_width:
            qb[:, b : b + 128] = done.astype(BF)
        else:
            kv_all[own_rows, b - q_width : b - q_width + 128] = done.astype(BF)

    q_slot = place.c * piece + lax.broadcasted_iota(jnp.int32, (rows, piece), 0)
    n_pairs = q_width // 128

    def one_piece(p):
        k_slot = p * piece + lanes((rows, piece))
        open_ = (k_slot >= start_col) & (k_slot <= q_slot)
        bias[...] = jnp.where(open_, 0.0, NEG_FILL)
        at = block_rows(p, piece)

        def heads_of(members):
            for g, (kb, ke), (vb, ve) in members:
                q2 = two_heads(qb[:, lane_block(g)])
                k2 = twice(kv_all[at, lane_block(kb)], ke)
                v2 = twice(kv_all[at, lane_block(vb)], ve)
                for h in range(2):
                    part = slice(h * rows, (h + 1) * rows)
                    e = jnp.exp(dot(q2[part], k2, 1, 1) * 0.125 + bias[...])
                    part_sum = e[:, :128]
                    for b in range(128, piece, 128):
                        part_sum = part_sum + e[:, b : b + 128]
                    acc[g, part, :] += dot(e.astype(BF), v2, 1, 0)
                    total[g, part, :] += part_sum

        over_key_heads(n_pairs, kv_width // HEAD_SIZE, heads_of)

    acc[...] = jnp.zeros_like(acc)
    total[...] = jnp.zeros_like(total)
    one_piece(place.c)
    x_bit, core_bit = place.c // 2, lax.rem(place.c, 2)
    near, across, passed = later
    first.advance(1)
    second.advance(1)

    @pl.when(x_bit == 1)
    def _():
        across.wait_recv()
        passed.start()

    first.from_chip(0)
    second.from_chip(0)
    tail.to_chip(0)
    first.to_chip(1)
    for copy in route_y:
        copy.wait_recv()
    own_y[...] = dot(pick[...], got_y[...], 1, 0).astype(BF)
    for copy in wide_y:
        copy.start()
    y_land[:, block_rows(place.t, feat)] = own_y[...]

    @pl.when(core_bit == 1)
    def _():
        near.wait_recv()
        one_piece(place.c - 1)

    first.advance(2)
    second.advance(2)
    second.to_chip(1)

    @pl.when(x_bit == 1)
    def _():
        passed.wait_recv()

        def step(p, carry):
            one_piece(p)
            return carry

        lax.fori_loop(0, 2, step, 0)

    ones = jnp.ones((8, 128), F32)
    for g in range(n_pairs):
        row_total = jnp.sum(total[g], axis=1, keepdims=True)
        heads[:, 128 * g : 128 * g + 128] = one_row(acc[g] / row_total)
        sums[g] = 1.0 / dot(ones, total[g], 1, 1, lax.Precision.HIGHEST)
    part[...] = dot(heads[...].astype(BF), w[:, q_width + 2 * kv_width :], 1, 1).astype(BF)
    attention = [
        remote(part, land.at[j - 1], tp_send.at[2, j], tp_recv.at[2, j], place.side(j))
        for j in range(1, tp)
    ]
    for copy in attention:
        copy.start()
    store(qb, qb_out)
    store(heads, heads_out)
    first.from_chip(1)
    first.to_chip(2)
    first.advance(3)
    second.advance(3)
    third.begin()
    tail.from_chip(0)
    tail.begin()
    tail.begin_other()
    second.from_chip(1)
    second.to_chip(2)
    first.from_chip(2)
    first.to_chip(3)
    third.advance(1)
    second.from_chip(2)
    second.to_chip(3)
    third.to_chip(0)
    tail.advance(1)
    third.advance(2)
    first.from_chip(3)
    third.to_chip(1)
    for copy in attention:
        copy.wait_recv()
    att = part[...].astype(F32)
    for j in range(1, tp):
        att = att + land[j - 1].astype(F32)
    v = x_land[...].astype(F32)
    squares[0:1, :] = jnp.sum(v * v, axis=0, keepdims=True)
    squares[1:2, :] = jnp.sum(att * att, axis=0, keepdims=True)
    mid[...] = v + att
    store(mid.at[:, block_rows(place.t, feat)], mid_own)
    v = (v + att).astype(BF).astype(F32)
    nb[...] = (v * row_scale(v) * gain_ffn[...]).astype(BF)
    store(nb, normed_two)
    ffn_acc[...] = jnp.zeros_like(ffn_acc)
    dn_acc[...] = jnp.zeros_like(dn_acc)
    third.to_chip(2)
    third.from_chip(0)
    for copy in wide_y:
        copy.wait_recv()
    store(y_land, dy)

    def one_tile(i):
        at = lambda m: block_rows(3 * i + m, tile)
        w_gate, w_up, w_down = w_ffn[:, at(0)], w_ffn[:, at(1)], w_ffn[:, at(2)]
        gate = dot(nb[...], w_gate, 1, 0)
        up = dot(nb[...], w_up, 1, 0)
        d_hidden = dot(y_land[...], w_down, 1, 0)
        sig = 1.0 / (1.0 + jnp.exp(-gate))
        silu = gate * sig
        out = block_rows(i, tile)
        acts[0, :, out] = (silu * up).astype(BF)
        acts[1, :, out] = (d_hidden * up * (sig * (1.0 + gate * (1.0 - sig)))).astype(BF)
        acts[2, :, out] = (d_hidden * silu).astype(BF)
        ffn_acc[...] += dot(acts[0, :, out], w_down, 1, 1)
        dn_acc[...] += dot(acts[1, :, out], w_gate, 1, 1) + dot(acts[2, :, out], w_up, 1, 1)

    act_stores = []
    for i, g in enumerate(groups + [tail]):
        if i == 1:
            tail.advance(2)
            third.advance(3)
            third.to_chip(3)
            second.from_chip(3)
            third.from_chip(1)
        if i == 2:
            tail.advance(3)
            third.from_chip(2)
            third.from_chip(3)
        g.finish()
        repeat(cuts[i + 1] - cuts[i], lambda k, i=i: one_tile(cuts[i] + k))
        cols = pl.ds(cuts[i] * tile, (cuts[i + 1] - cuts[i]) * tile)
        for m, out in enumerate((hidden, d_gate, d_up)):
            copy = pltpu.make_async_copy(acts.at[m, :, cols], out.at[:, cols], act_sem.at[m, i])
            copy.start()
            act_stores.append(copy)
    dgain[...] = jnp.zeros_like(dgain)

    def finish_rows(i):
        r = block_rows(i, 128)
        v = mid[r, :].astype(BF).astype(F32)
        grad, gain_sum = norm_back(dn_acc[r, :], v, gain_ffn[...])
        dgain[...] += gain_sum
        dmid[r, :] = grad.astype(BF)
        ffn_out[r, :] = ffn_acc[r, :].astype(BF)

    repeat(rows // 128, finish_rows)

    @pl.when(core_bit == 0)
    def _():
        near.wait_send()

    @pl.when(x_bit == 0)
    def _():
        across.wait_send()

    @pl.when(x_bit == 1)
    def _():
        passed.wait_send()

    store(kv_all, kv)
    for copy in route_x + route_y + wide_x + wide_y + attention:
        copy.wait_send()
    for g in [attn, tail] + groups:
        g.drain()
    for copy in stores + act_stores:
        copy.wait()


def start_keys(place, kv_all, own_rows, send, recv):
    x_bit, core_bit = place.c // 2, lax.rem(place.c, 2)
    mine = kv_all.at[own_rows, :]
    near = remote(mine, mine, send.at[0], recv.at[0], place.at(c=place.flip(1)))
    across = remote(mine, mine, send.at[1], recv.at[1], place.at(c=place.flip(2)))
    from_chip = kv_all.at[block_rows(place.flip(2), own_rows.size), :]
    passed = remote(from_chip, from_chip, send.at[2], recv.at[2], place.at(c=place.flip(1)))

    @pl.when(x_bit == 0)
    def _():
        across.start()

    @pl.when(core_bit == 0)
    def _():
        near.start()

    return near, across, passed


def forward_pass(grid, q_width, kv_width, tile, *operands):
    tokens, w_query, w_key, w_gate = operands[1], operands[8], operands[9], operands[12]
    rows, feat = tokens.shape
    n, ctx, tp = grid.n, grid.ctx, grid.tp
    width = feat * tp
    n_pairs = q_width // 128
    row_len = rows * ctx
    ff = -(-w_gate.shape[1] // tile) * tile
    vm = pl.BlockSpec(memory_space=pltpu.VMEM)
    dma = pltpu.SemaphoreType.DMA
    V = pltpu.VMEM
    group = n * ctx
    attn_width = 2 * w_query.shape[1] + 2 * w_key.shape[1]
    return pl.pallas_call(
        functools.partial(forward_kernel, n, ctx, tp, q_width, kv_width, tile),
        in_specs=[pl.BlockSpec(memory_space=pltpu.SMEM)] + [vm] * 14,
        out_specs=[vm] * 9 + [ANYWHERE] * 11,
        out_shape=[
            shape((n_pairs, 8, 2 * rows), F32),
            shape((2, width), F32),
            shape((rows, width), BF),
            shape((rows, width), BF),
            shape((1, width), F32),
            shape((rows, rows), BF),
            shape((rows, rows), BF),
            shape((rows, 128), F32),
            shape((rows, 128), F32),
            shape((rows, width), BF),
            shape((rows, width), BF),
            shape((rows, q_width), BF),
            shape((row_len, 2 * kv_width), BF),
            shape((rows, q_width), F32),
            shape((rows, feat), F32),
            shape((width, attn_width), BF),
            shape((rows, width), BF),
            shape((rows, ff), BF),
            shape((rows, ff), BF),
            shape((rows, ff), BF),
        ],
        scratch_shapes=[V((rows, feat), BF)] * 6
        + [
            V((rows, width), BF),
            V((rows, width), BF),
            V((rows, rows), BF),
            V((rows, q_width), BF),
            V((rows, q_width), F32),
            V((rows, width), F32),
            V((rows, width), BF),
            V((width, attn_width), BF),
            V((width, 3 * ff), BF),
            V((row_len, 2 * kv_width), BF),
            V((rows, width), BF),
            V((tp - 1, rows, width), BF),
            V((n_pairs, 2 * rows, 128), F32),
            V((n_pairs, 2 * rows, 128), F32),
            V((rows, rows), F32),
            V((rows, width), F32),
            V((rows, width), F32),
            V((3, rows, ff), BF),
            dma((2, group)),
            dma((2, group)),
            dma((3, tp)),
            dma((3, tp)),
            dma((3,)),
            dma((3,)),
            dma((8,)),
            dma((3, 4)),
            dma((6, n)),
            dma((6, n)),
            dma((5, n)),
            dma((5, n)),
            dma((5, 2 * n)),
            dma((5, 2 * n)),
        ],
        compiler_params=pltpu.CompilerParams(
            vmem_limit_bytes=61 * 2**20, collective_id=0, has_side_effects=True
        ),
        cost_estimate=pl.CostEstimate(
            flops=12 * rows * width * ff, bytes_accessed=40 * 2**20, transcendentals=0
        ),
    )(*operands)


def repeat(count, body):
    def step(i, carry):
        body(i)
        return carry

    lax.fori_loop(0, count, step, 0)


def add_into(to, more):
    step = 16

    def add(i):
        at = block_rows(i, step)
        to[at, :] = (to[at, :].astype(F32) + more[at, :].astype(F32)).astype(to.dtype)

    repeat(to.shape[0] // step, add)


def turn_blocks(place, source, turned):
    width = source.shape[1]
    n = place.n
    h = width // (n * place.ctx)
    first = lax.rem(place.c, 2) == 0

    def turn(i):
        chip = lax.rem(place.c // 2 + i // n, 2)
        pair = lax.rem(place.z - lax.rem(i, n) + n, n) * (place.ctx // 2) + chip
        block = source[:, block_rows(pair, 2 * h)].astype(F32).T.astype(turned.dtype)
        low, high = block[:h], block[h:]
        turned[block_rows(i, h), :] = jnp.where(first, low, high)
        turned[block_rows(i + 2 * n, h), :] = jnp.where(first, high, low)

    repeat(2 * n, turn)


class Scatter:
    def __init__(
        self, place, keep, columns, chip_land, line_land, number, sems, line_first=False
    ):
        x_send, x_recv, z_send, z_recv = sems
        n = place.n
        self.n, self.line_first = n, line_first
        self.h = h = keep.shape[0] // (2 * n)
        self.keep = [keep.at[pl.ds(k * h, h), columns] for k in range(2 * n)]
        land = [chip_land.at[pl.ds(k * h, h), columns] for k in range(n)]
        line = [line_land.at[k, :, columns] for k in range(n - 1)]
        there = place.at(c=place.flip(2))

        def ring(blocks, lands, row):
            return [
                remote(blocks[k], lands[k - 1], z_send.at[row, k], z_recv.at[row, k], place.up(1))
                for k in range(1, n)
            ]

        self.rings = [(ring(self.keep[:n], line, number), self.keep[:n], line)]
        if line_first:
            self.rings.append((ring(self.keep[n:], land[1:], number + 1), self.keep[n:], land[1:]))
            self.chip = remote(
                self.keep[n], land[0], x_send.at[number], x_recv.at[number], there
            )
            self.chip_land = land[:1]
        else:
            self.chip = remote(
                keep.at[pl.ds(n * h, n * h), columns],
                chip_land.at[:, columns],
                x_send.at[number],
                x_recv.at[number],
                there,
            )
            self.chip_land = land

    def to_chip(self):
        self.chip.start()

    def from_chip(self):
        self.chip.wait_recv()
        if self.line_first:
            return
        for k in list(range(1, self.n)) + [0]:
            add_into(self.keep[k], self.chip_land[k])
            if k == 1:
                self.begin()

    def begin(self):
        for ring, _, _ in self.rings:
            if ring:
                ring[0].start()

    def advance(self, k):
        if k >= self.n:
            return
        for ring, blocks, lands in self.rings:
            ring[k - 1].wait_recv()
            if k + 1 < self.n:
                add_into(blocks[k + 1], lands[k - 1])
                ring[k].start()
            elif self.line_first:
                add_into(blocks[0], lands[k - 1])

    def finish(self, out):
        last = self.chip_land[0] if self.line_first else self.rings[0][2][self.n - 2]
        step = 16

        def add(i):
            at = block_rows(i, step)
            out[at, :] = self.keep[0][at, :].astype(F32) + last[at, :].astype(F32)

        repeat(self.h // step, add)

    def drain(self):
        self.chip.wait_send()
        for ring, _, _ in self.rings:
            for copy in ring:
                copy.wait_send()


def core_sum(keep, core_land, copy):
    copy.wait_recv()
    add_into(keep, core_land)


def backward_kernel(
    n, ctx, tp, q_width, kv_width, stage_cols,
    lengths, ffn, dmid, sums, cosines, sines, pick_t, gain, head_gain,
    gain_ffn_grad, squares, qb_in, kv_in, heads_in, w_in, dy_in, x_in, mid_in, normed_two, hidden, d_gate, d_up,
    back_o, back_g, sum_gate, sum_up, sum_down, sum_out, sum_qkv, small,
    qb, kv_all, heads, w, x, turned, stage, keep, send, core_land, chip_land, line_land,
    o_keep, o_send, o_core, o_chip, o_line, a_keep, a_send, a_core, a_chip, a_line,
    d_mid_own, d_attn, dob, delta, bias, dq_t, dkv, kv_land, tp_land, ffn_away, ffn_land, dx_away, dx_land,
    sent, small_mine, small_land, small_side,
    tp_send, tp_recv, route_send, route_recv, small_send, small_recv, kv_send, kv_recv, load_sem,
    free_sem, *scatter_sems
):
    place = Place(n, ctx, tp)
    group = n * ctx
    rows, width = dmid.shape
    feat = width // tp
    share = rows // group
    piece = rows
    ff = hidden.shape[1]
    half = width // 2
    n_pairs = q_width // 128
    qkv_width = q_width + 2 * kv_width
    values_from = q_width + kv_width
    x_bit, core_bit = place.c // 2, lax.rem(place.c, 2)
    own_cols = block_rows(place.t, feat)
    c_send, c_recv, *ring_sems = scatter_sems
    everything = pl.ds(0, ff)
    lands = lambda m: (chip_land.at[m], line_land.at[m])
    cut = ff // 128 * 11 // 18 * 128
    down = Scatter(place, keep.at[0], pl.ds(0, cut), *lands(0), 0, ring_sems, True)
    down_x = Scatter(place, keep.at[0], pl.ds(cut, ff - cut), *lands(0), 6, ring_sems)
    gate = Scatter(place, keep.at[1], everything, *lands(1), 2, ring_sems)
    up = Scatter(place, keep.at[2], everything, *lands(2), 3, ring_sems)
    out_sum = Scatter(place, o_keep, pl.ds(0, q_width), o_chip, o_line, 4, ring_sems)
    qkv_sum = Scatter(place, a_keep, pl.ds(0, qkv_width), a_chip, a_line, 5, ring_sems)
    across_cores = [
        remote(src, dst, c_send.at[i], c_recv.at[i], place.at(c=place.flip(1)))
        for i, (src, dst) in enumerate(
            [(send.at[m % 2], core_land.at[m % 2]) for m in range(3)]
            + [(o_send, o_core), (a_send, a_core)]
        )
    ]

    def to_sides(number, src, dst):
        return [
            remote(
                src(j), dst.at[j - 1], tp_send.at[number, j], tp_recv.at[number, j], place.side(j)
            )
            for j in range(1, tp)
        ]

    def away(buffer):
        return lambda j: buffer.at[j - 1]

    def fill_away(buffer, source):
        for j in range(1, tp):
            buffer[j - 1] = source[:, block_rows(lax.rem(place.t + j, tp), feat)]

    def route(number, src, dst):
        return [
            remote(
                src.at[block_rows(lax.rem(place.me + j, group), share), :],
                dst.at[block_rows(place.me, share), :],
                route_send.at[number, j],
                route_recv.at[number, j],
                place.peer(j),
            )
            for j in range(1, group)
        ]

    dmid_sum = to_sides(0, lambda j: dmid, tp_land)
    ffn_sum = to_sides(1, away(ffn_away), ffn_land)
    dx_sum = to_sides(2, away(dx_away), dx_land)
    route_o, route_g = route(0, sent, back_o), route(1, dob, back_g)

    place.greet()
    for copy in dmid_sum:
        copy.start()

    sources = (hidden, d_gate, d_up)
    tiles = [(m, b) for m in range(3) for b in range(0, ff, stage_cols)]
    loads = [
        pltpu.make_async_copy(
            sources[m].at[:, pl.ds(b, stage_cols)], stage.at[i % 2], load_sem.at[i]
        )
        for i, (m, b) in enumerate(tiles)
    ]
    load_n = pltpu.make_async_copy(normed_two, d_attn, load_sem.at[len(tiles)])
    dy, mid = x, d_mid_own
    load_dy = pltpu.make_async_copy(dy_in, dy, load_sem.at[len(tiles) + 1])
    load_x = pltpu.make_async_copy(x_in, x, load_sem.at[len(tiles) + 2])
    load_mid = pltpu.make_async_copy(mid_in, mid, load_sem.at[len(tiles) + 3])
    load_dy.start()
    loads[0].start()
    load_n.start()
    load_mid.start()
    more_loads = [
        pltpu.make_async_copy(src, dst, load_sem.at[len(tiles) + 5 + i])
        for i, (src, dst) in enumerate(((w_in, w), (qb_in, qb), (kv_in, kv_all), (heads_in, heads)))
    ]
    for copy in more_loads:
        copy.start()
    fill_away(ffn_away, ffn)
    load_dy.wait()
    turn_blocks(place, dy, turned)
    sub = 256 if stage_cols % 256 == 0 else 128
    for i, (m, b) in enumerate(tiles):
        if i + 1 < len(tiles):
            loads[i + 1].start()
        if b == 0 and m == 1:
            load_n.wait()
            turn_blocks(place, d_attn, turned)
        if m == 1 and b == ff // 2 // stage_cols * stage_cols:
            core_sum(keep.at[0], core_land.at[0], across_cores[0])
            down.begin()
            down_x.to_chip()
            pl.semaphore_signal(
                free_sem, inc=1, device_id=place.at(c=place.flip(1)), device_id_type=MESH
            )
        if b == 0 and m == 2:
            across_cores[0].wait_send()
        if m == 2 and b == ff // 2 // stage_cols * stage_cols:
            core_sum(keep.at[1], core_land.at[1], across_cores[1])
            gate.to_chip()
        loads[i].wait()
        for s in range(0, stage_cols, sub):
            right = stage[i % 2, :, s : s + sub]
            cols = slice(b + s, b + s + sub)
            keep[m, :, cols] = dot(turned[:half, :], right, 1, 0).astype(BF)
            send[m % 2, :, cols] = dot(turned[half:, :], right, 1, 0).astype(BF)
        if b + stage_cols == ff:
            if m == 2:
                pl.semaphore_wait(free_sem, 1)
            across_cores[m].start()
    core_sum(keep.at[2], core_land.at[0], across_cores[2])

    for copy in more_loads:
        copy.wait()
    for copy in dmid_sum:
        copy.wait_recv()
    for copy in ffn_sum:
        copy.start()

    def sum_gradient(i):
        r = block_rows(i, 128)
        d_all = dy[r, :].astype(F32) + dmid[r, :].astype(F32)
        for j in range(1, tp):
            d_all = d_all + tp_land[j - 1, r, :].astype(F32)
        d_attn[r, :] = d_all.astype(BF)

    repeat(rows // 128, sum_gradient)
    dob[...] = dot(d_attn[...], w[:, qkv_width:], 1, 0).astype(BF)
    dq_t[...] = jnp.zeros_like(dq_t)
    ones = jnp.ones((8, 128), F32)

    def set_delta(g):
        both = dob[:, lane_block(g)].astype(F32) * heads[:, lane_block(g)]
        delta[g] = dot(ones, two_heads(both), 1, 1, lax.Precision.HIGHEST)

    repeat(n_pairs, set_delta)
    q_slot = place.c * piece + lanes((piece, rows))
    start_row = segment_start(lengths, place.c * piece + lanes((8, rows)))[:1]

    def one_piece(p):
        k_slot = p * piece + lax.broadcasted_iota(jnp.int32, (piece, rows), 0)
        open_ = (k_slot >= start_row) & (k_slot <= q_slot)
        bias[...] = jnp.where(open_, 0.0, NEG_FILL)
        at = block_rows(p, piece)
        def heads_of(members):
            grads = []
            for g, (kb, ke), (vb, ve) in members:
                q2 = two_heads(qb[:, lane_block(g)])
                do2 = two_heads(dob[:, lane_block(g)])
                k2 = twice(kv_all[at, lane_block(kb)], ke)
                v2 = twice(kv_all[at, lane_block(vb)], ve)
                k_t = k2.astype(F32).T.astype(BF)
                dk = jnp.zeros((piece, 128), F32)
                dv = jnp.zeros((piece, 128), F32)
                for h in range(0, 2 * rows, 256):
                    part = slice(h, h + 256)
                    open_part = slice(h % rows, h % rows + 256)
                    s = dot(k2, q2[part], 1, 1)
                    dp = dot(v2, do2[part], 1, 1)
                    pe = jnp.exp(s * 0.125 + bias[:, open_part]) * sums[g, 0:1, part]
                    ds = (pe * (dp - delta[g, 0:1, part])).astype(BF)
                    dv = dv + dot(pe.astype(BF), do2[part], 1, 0)
                    dk = dk + dot(ds, q2[part], 1, 0)
                    dq_t[g, :, part] += dot(k_t, ds, 1, 0)
                grads.append((both_halves(dk) * 0.125, both_halves(dv)))
            low = lanes((piece, 128)) < HEAD_SIZE
            kb, vb = members[0][1][0], members[0][2][0]
            if len(members) == 2:
                dkv[at, lane_block(kb)] = jnp.where(low, grads[0][0], grads[1][0]).astype(BF)
                dkv[at, lane_block(vb)] = jnp.where(low, grads[0][1], grads[1][1]).astype(BF)
            else:
                for value, (b, e) in zip(grads[0], members[0][1:]):
                    c = 128 * b + HEAD_SIZE * e
                    dkv[at, c : c + HEAD_SIZE] = value[:, :HEAD_SIZE].astype(BF)

        over_key_heads(n_pairs, kv_width // HEAD_SIZE, heads_of)

    down.advance(1)
    down_x.from_chip()

    sibling = place.at(c=place.flip(1))
    other = 1 - core_bit
    to_passer = remote(
        dkv.at[block_rows(other, piece), :], kv_land.at[0], kv_send.at[0], kv_recv.at[0], sibling
    )
    to_chip = remote(
        dkv.at[block_rows(core_bit, piece), :],
        kv_land.at[0],
        kv_send.at[1],
        kv_recv.at[1],
        place.at(c=place.flip(2)),
    )
    to_core = remote(
        dkv.at[block_rows(2 * x_bit, piece), :], kv_land.at[1], kv_send.at[2], kv_recv.at[2], sibling
    )

    @pl.when(x_bit == 1)
    def _():
        def step(p, carry):
            one_piece(p)
            return carry

        lax.fori_loop(0, 2, step, 0)
        to_passer.start()

    turn_blocks(place, d_attn, turned)
    right = heads[...].astype(BF)
    o_keep[...] = dot(turned[:half, :], right, 1, 0).astype(BF)
    o_send[...] = dot(turned[half:, :], right, 1, 0).astype(BF)
    across_cores[3].start()
    down.advance(2)
    down_x.advance(1)

    @pl.when(x_bit == 1)
    def _():
        to_passer.wait_recv()
        mine = block_rows(core_bit, piece)
        dkv[mine, :] = (dkv[mine, :].astype(F32) + kv_land[0].astype(F32)).astype(BF)
        to_chip.start()

    gate.from_chip()

    @pl.when(x_bit == 0)
    def _():
        up.to_chip()

    core_sum(o_keep, o_core, across_cores[3])
    out_sum.to_chip()

    @pl.when(core_bit == 1)
    def _():
        one_piece(place.c - 1)
        to_core.start()

    for copy in ffn_sum:
        copy.wait_recv()
    small_mine[...] = jnp.zeros_like(small_mine)
    load_mid.wait()

    def finish_output(i):
        r = block_rows(i, 128)
        ffn_out = ffn[r, own_cols].astype(F32)
        for j in range(1, tp):
            ffn_out = ffn_out + ffn_land[j - 1, r, :].astype(F32)
        small_mine[5:6, :feat] += jnp.sum(ffn_out * ffn_out, axis=0, keepdims=True)
        dx_away[0, r, :] = (mid[r, :] + ffn_out).astype(BF)

    repeat(rows // 128, finish_output)
    sent[...] = dot(pick_t[...], dx_away[0], 1, 0).astype(BF)
    for copy in route_o:
        copy.start()
    own = block_rows(place.me, share)
    back_o[own, :] = sent[own, :]


    def own_gradient(i):
        r = block_rows(i, 128)
        d_own = dy[r, own_cols].astype(F32) + dmid[r, own_cols].astype(F32)
        for j in range(1, tp):
            d_own = d_own + tp_land[j - 1, r, own_cols].astype(F32)
        d_mid_own[r, :] = d_own

    repeat(rows // 128, own_gradient)
    load_x.start()

    @pl.when(x_bit == 1)
    def _():
        to_chip.wait_send()
        up.to_chip()

    one_piece(place.c)
    down.advance(3)
    down.to_chip()
    down_x.advance(2)
    gate.advance(1)
    normed = tp_land.at[0]
    load_x.wait()

    def norm_again(i):
        v = x[block_rows(i, 128), :].astype(F32)
        normed[block_rows(i, 128), :] = (v * row_scale(v) * gain[...]).astype(BF)

    repeat(rows // 128, norm_again)
    turn_blocks(place, normed, turned)
    mine = block_rows(place.c, piece)

    @pl.when(core_bit == 0)
    def _():
        to_core.wait_recv()

    @pl.when(x_bit == 0)
    def _():
        to_chip.wait_recv()

    d_qkv = d_attn.at[:, pl.ds(0, qkv_width)]
    for b in range(0, qkv_width, 128):
        if b < q_width:
            g = b // 128
            grad = one_row(dq_t[g].T) * 0.125
        else:
            cols = slice(b - q_width, b - q_width + 128)
            grad = dkv[mine, cols].astype(F32)
            grad = jnp.where(x_bit == 0, grad + kv_land[0, :, cols].astype(F32), grad)
            grad = jnp.where(core_bit == 0, grad + kv_land[1, :, cols].astype(F32), grad)
        raw = dot(normed[...], w[:, b : b + 128], 1, 0)
        is_value = lanes(grad.shape) + b >= values_from
        back, gain_grad = qk_backward(
            grad, raw, head_gain[:, b : b + 128], cosines[...], sines[...], is_value
        )
        small_mine[2:3, b : b + 128] = gain_grad
        d_qkv[:, b : b + 128] = back.astype(BF)

    def finish_gradient(i):
        r = block_rows(i, 128)
        dn = dot(d_qkv[r, :], w[:, :qkv_width], 1, 1)
        dx, gain_grad = norm_back(dn, x[r, :].astype(F32), gain[...])
        normed[r, :] = dx.astype(BF)
        small_mine[0:1, :] += gain_grad

    repeat(rows // 128, finish_gradient)
    fill_away(dx_away, normed)
    for copy in dx_sum:
        copy.start()
    small_mine[1:2, :] = gain_ffn_grad[...]
    small_mine[3:5, :] = squares[...]
    for b in range(0, qkv_width, 256):
        cols = slice(b, b + 256)
        a_keep[:, cols] = dot(turned[:half, :], d_qkv[:, cols], 1, 0).astype(BF)
        a_send[:, cols] = dot(turned[half:, :], d_qkv[:, cols], 1, 0).astype(BF)
    across_cores[4].start()
    down_x.advance(3)
    gate.advance(2)
    small_out = [
        remote(
            small_mine, small_land.at[place.me], small_send.at[0, j], small_recv.at[0, j], place.peer(j)
        )
        for j in range(1, group)
    ]
    for copy in small_out:
        copy.start()
    small_land[place.me] = small_mine[...]
    core_sum(a_keep, a_core, across_cores[4])
    qkv_sum.to_chip()
    out_sum.from_chip()
    up.from_chip()

    for copy in dx_sum:
        copy.wait_recv()
    for copy in ffn_sum:
        copy.wait_send()

    def finish_input(i):
        r = block_rows(i, 128)
        total = d_mid_own[r, :] + normed[r, own_cols].astype(F32)
        for j in range(1, tp):
            total = total + dx_land[j - 1, r, :].astype(F32)
        ffn_away[0, r, :] = total.astype(BF)

    repeat(rows // 128, finish_input)
    dob[...] = dot(pick_t[...], ffn_away[0], 1, 0).astype(BF)
    for copy in route_g:
        copy.start()
    back_g[own, :] = dob[own, :]
    gate.advance(3)
    out_sum.advance(1)
    up.advance(1)
    qkv_sum.from_chip()
    gate.finish(sum_gate)
    out_sum.advance(2)
    up.advance(2)
    qkv_sum.advance(1)
    down.from_chip()
    down.finish(sum_down.at[:, pl.ds(0, cut)])
    down_x.finish(sum_down.at[:, pl.ds(cut, ff - cut)])
    out_sum.advance(3)
    up.advance(3)
    qkv_sum.advance(2)
    out_sum.finish(sum_out)
    up.finish(sum_up)
    for copy in small_out:
        copy.wait_recv()
    total = small_land[0]
    for i in range(1, group):
        total = total + small_land[i]
    small_side[place.t] = total
    for copy in small_out:
        copy.wait_send()
    small_mine[...] = total
    sides = [
        remote(
            small_mine, small_side.at[place.t], small_send.at[1, j], small_recv.at[1, j], place.side(j)
        )
        for j in range(1, tp)
    ]
    for copy in sides:
        copy.start()
    for copy in sides:
        copy.wait_recv()
    total = small_side[0]
    for j in range(1, tp):
        total = total + small_side[j]
    small[...] = total
    for copy in route_o:
        copy.wait_recv()
    qkv_sum.advance(3)
    qkv_sum.finish(sum_qkv)
    for copy in route_g:
        copy.wait_recv()

    @pl.when(x_bit == 1)
    def _():
        to_passer.wait_send()

    @pl.when(core_bit == 1)
    def _():
        to_core.wait_send()

    for copy in dmid_sum + dx_sum + route_o + route_g + sides:
        copy.wait_send()
    for copy in across_cores[1:]:
        copy.wait_send()
    for s in (down, down_x, gate, up, out_sum, qkv_sum):
        s.drain()


def backward_pass(grid, q_width, kv_width, *operands):
    dmid, hidden = operands[2], operands[19]
    rows, width = dmid.shape
    ff = hidden.shape[1]
    n, ctx, tp = grid.n, grid.ctx, grid.tp
    group = n * ctx
    feat = width // tp
    half = width // 2
    h = width // group
    n_pairs = q_width // 128
    qkv_width = q_width + 2 * kv_width
    stage_cols = 256 if ff % 256 == 0 else 128
    vm = pl.BlockSpec(memory_space=pltpu.VMEM)
    dma = pltpu.SemaphoreType.DMA
    V = pltpu.VMEM

    def scatter_space(cols):
        return [
            V((half, cols), BF),
            V((half, cols), BF),
            V((half, cols), BF),
            V((half // 2, cols), BF),
            V((n - 1, h, cols), BF),
        ]

    return pl.pallas_call(
        functools.partial(backward_kernel, n, ctx, tp, q_width, kv_width, stage_cols),
        in_specs=[pl.BlockSpec(memory_space=pltpu.SMEM)] + [vm] * 10 + [ANYWHERE] * 11,
        out_specs=[vm] * 8,
        out_shape=[
            shape((rows, feat), BF),
            shape((rows, feat), BF),
            shape((h, ff), F32),
            shape((h, ff), F32),
            shape((h, ff), F32),
            shape((h, q_width), F32),
            shape((h, qkv_width), F32),
            shape((8, width), F32),
        ],
        scratch_shapes=[
            V((rows, q_width), BF),
            V((rows * ctx, 2 * kv_width), BF),
            V((rows, q_width), F32),
            V((width, q_width + qkv_width), BF),
            V((rows, width), BF),
            V((width, rows), BF),
            V((2, rows, stage_cols), BF),
            V((3, half, ff), BF),
            V((2, half, ff), BF),
            V((2, half, ff), BF),
            V((3, half // 2, ff), BF),
            V((3, n - 1, h, ff), BF),
        ]
        + scatter_space(q_width)
        + scatter_space(qkv_width)
        + [
            V((rows, feat), F32),
            V((rows, width), BF),
            V((rows, q_width), BF),
            V((n_pairs, 8, 2 * rows), F32),
            V((rows, rows), F32),
            V((n_pairs, 128, 2 * rows), F32),
            V((rows * ctx, 2 * kv_width), BF),
            V((2, rows, 2 * kv_width), BF),
            V((tp - 1, rows, width), BF),
            V((tp - 1, rows, feat), BF),
            V((tp - 1, rows, feat), BF),
            V((tp - 1, rows, feat), BF),
            V((tp - 1, rows, feat), BF),
            V((rows, feat), BF),
            V((8, width), F32),
            V((group, 8, width), F32),
            V((tp, 8, width), F32),
            dma((3, tp)),
            dma((3, tp)),
            dma((2, group)),
            dma((2, group)),
            dma((2, max(group, tp))),
            dma((2, max(group, tp))),
            dma((3,)),
            dma((3,)),
            dma((3 * (ff // stage_cols) + 9,)),
            pltpu.SemaphoreType.REGULAR,
            dma((5,)),
            dma((5,)),
            dma((7,)),
            dma((7,)),
            dma((7, n)),
            dma((7, n)),
        ],
        compiler_params=pltpu.CompilerParams(
            vmem_limit_bytes=61 * 2**20, collective_id=1, has_side_effects=True
        ),
        cost_estimate=pl.CostEstimate(
            flops=20 * rows * rows * ctx * q_width, bytes_accessed=40 * 2**20, transcendentals=0
        ),
    )(*operands)


def output_kernel(
    tp, entries, place_o, place_g, send_back, gate, up, down, out, qkv, small,
    output, grad_tokens, g_query, g_key, g_value, g_out, g_gate, g_up, g_down,
    gain_a, gain_f, gain_q, gain_k, stats
):
    a, b = g_query.shape[1], g_query.shape[1] + g_key.shape[1]
    output[...] = dot(send_back[...], place_o[...], 1, 0).astype(BF)
    grad_tokens[...] = dot(send_back[...], place_g[...], 1, 0).astype(BF)
    g_query[...] = qkv[:, :a]
    g_key[...] = qkv[:, a:b]
    g_value[...] = qkv[:, b:]
    g_out[...] = out[...]
    ff = g_gate.shape[1]
    g_gate[...] = gate[:, :ff]
    g_up[...] = up[:, :ff]
    g_down[...] = down[:, :ff]
    gain_a[...] = small[0:1, :]
    gain_f[...] = small[1:2, :]

    def heads_sum(first, last):
        total = jnp.zeros((1, HEAD_SIZE), F32)
        for c in range(first, last, HEAD_SIZE):
            total = total + small[2:3, c : c + HEAD_SIZE]
        return total

    gain_q[...] = heads_sum(0, a)
    gain_k[...] = heads_sum(a, b)
    row = lanes((1, 128))
    x_sum, attn_sum, ffn_sum = (
        jnp.sum(small[3 + i : 4 + i, :], axis=1, keepdims=True) for i in range(3)
    )
    total = jnp.where(row == 0, x_sum / tp, jnp.where(row == 1, attn_sum / tp, ffn_sum))
    stats[...] = jnp.sqrt(total * (1.0 / entries))


def output_pass(grid, shapes, *operands):
    rows = operands[0].shape[0]
    entries = rows * grid.n * grid.ctx * MODEL_WIDTH
    row = lambda n: shape((1, n), F32)
    vm = pl.BlockSpec(memory_space=pltpu.VMEM)
    outs = (
        [shape(operands[0].shape, BF)] * 2
        + [shape(s, F32) for s in shapes]
        + [row(MODEL_WIDTH), row(MODEL_WIDTH), row(HEAD_SIZE), row(HEAD_SIZE), row(128)]
    )
    return pl.pallas_call(
        functools.partial(output_kernel, grid.tp, entries),
        in_specs=[vm] * len(operands),
        out_specs=[vm] * len(outs),
        out_shape=outs,
        compiler_params=pltpu.CompilerParams(vmem_limit_bytes=60 * 2**20),
    )(*operands)


def local(
    tokens,
    cotangent,
    slot_of,
    lengths,
    w_query,
    key_weight,
    value_weight,
    w_out,
    w_gate,
    w_up,
    w_down,
    gain_attn,
    gain_ffn,
    gain_query,
    gain_key,
):
    grid = Grid()
    rows, feat_len = tokens.shape
    q_heads = QUERY_HEADS // grid.tp
    key_value_heads = KEY_VALUE_HEADS // grid.tp
    q_width = q_heads * HEAD_SIZE
    kv_width = key_value_heads * HEAD_SIZE
    ff = w_gate.shape[1]
    tile = 256 if ff % 256 == 0 else 128
    head_gain = jnp.concatenate(
        [
            jnp.tile(gain_query, q_heads),
            jnp.tile(gain_key, key_value_heads),
            jnp.ones((kv_width,), F32),
        ]
    )[None, :]
    frequency = ROPE_THETA ** (-np.arange(0, HEAD_SIZE, 2, dtype=np.float64) / HEAD_SIZE)
    frequency = jnp.asarray(np.tile(frequency, 4)[None, :], F32)
    (
        sums, squares, ffn_part, d_mid_part, d_gain_ffn, take_back, send_back, cosines, sines,
        x_full, dy_full, qb, row_kv, heads, middle_own, attn_w, normed_two, hidden, d_gate, d_up,
    ) = forward_pass(
        grid,
        q_width,
        kv_width,
        tile,
        lengths,
        tokens,
        cotangent,
        slot_of.reshape(-1, 128),
        gain_attn[None, :],
        head_gain,
        gain_ffn[None, :],
        frequency,
        w_query,
        key_weight,
        value_weight,
        w_out.T,
        w_gate,
        w_up,
        w_down.T,
    )
    place_o, place_g, sum_gate, sum_up, sum_down, sum_out, sum_qkv, small = backward_pass(
        grid,
        q_width,
        kv_width,
        lengths,
        ffn_part,
        d_mid_part,
        sums,
        cosines,
        sines,
        take_back,
        gain_attn[None, :],
        head_gain,
        d_gain_ffn,
        squares,
        qb,
        row_kv,
        heads,
        attn_w,
        dy_full,
        x_full,
        middle_own,
        normed_two,
        hidden,
        d_gate,
        d_up,
    )
    weights = (w_query, key_weight, value_weight, w_out.T, w_gate, w_up, w_down.T)
    *outs, gain_a, gain_f, gain_q, gain_k, stats = output_pass(
        grid,
        [v.shape for v in weights],
        place_o,
        place_g,
        send_back,
        sum_gate,
        sum_up,
        sum_down,
        sum_out,
        sum_qkv,
        small,
    )
    outs[5], outs[8] = outs[5].T, outs[8].T
    return (*outs, gain_a[0], gain_f[0], gain_q[0], gain_k[0], stats[0, :3])


def solution(mesh):
    row = P(("fsdp", "ctx"), "tp")
    column = P("tp", ("fsdp", "ctx"))
    in_specs = (row, row, P(), P("fsdp", None), row, row, row, column, row, row, column) + (P(),) * 4
    out_specs = (row, row, row, row, row, column, row, row, column) + (P(),) * 5
    return jax.shard_map(local, mesh=mesh, in_specs=in_specs, out_specs=out_specs, check_vma=False)
```

profile of v0, /device:TPU:0, one launch (start us, length us, event | category | flops | bytes accessed | tf_op | source)
XLA Modules:
  0.0 317.0 jit_solution(9348322941407774438)
XLA Ops:
  0.6 0.7 tile.20
  1.3 0.1 tile.21
  1.4 0.7 tile.8
  2.0 0.1 tile.9
  2.1 0.6 pad_maximum_fusion
  2.7 149.7 %shard_map.263 = (f32[4,8,1024]{2,1,0:T(8,128)}, f32[2,1024]{1,0:T(2,128)}, bf16[512,1024]{1,0:T(8,128)(2,1)}, bf16[512,1024]{1,0:T(8,128)(2,1)}, f32[1,1024]{1,...) custom-call(s32[1,3]{1,0:T(1,128)} %lengths.3, ...), custom_call_target="tpu_custom_call" | custom-call | flops 14495514624 | bytes 41943040 | tf_op jit(solution)/shard_map/pallas_call | solution.py:692
  152.4 158.9 %shard_map.264 = (bf16[512,512]{1,0:T(8,128)(2,1)}, bf16[512,512]{1,0:T(8,128)(2,1)}, f32[64,2304]{1,0:T(8,128)}, f32[64,2304]{1,0:T(8,128)}, f32[64,2304]{1,0:T...) custom-call(s32[1,3]{1,0:T(1,128)} %lengths.3, bf16[512,1024]{1,0:T(8,128)(2,1)} %get-tuple-element.56.ffn, ...), custom_call_target="tpu_custom_call" | custom-call | flops 10737418240 | bytes 41943040 | tf_op jit(solution)/shard_map/pallas_call | solution.py:1357
  311.4 4.3 %shard_map.265 = (bf16[512,512]{1,0:T(8,128)(2,1)}, bf16[512,512]{1,0:T(8,128)(2,1)}, f32[64,512]{1,0:T(8,128)}, f32[64,256]{1,0:T(8,128)}, f32[64,256]{1,0:T(8,...) custom-call(bf16[512,512]{1,0:T(8,128)(2,1)} %get-tuple-element.75.p, ...), custom_call_target="tpu_custom_call" | custom-call | tf_op jit(solution)/shard_map/pallas_call | solution.py:1476
  315.7 1.1 slice_bitcast_fusion
  (1 shorter events, 0.0 us)
where the time goes:
time: 321 us; the launch traced here: 317 us
  Pallas kernels  313 us (98%)
    pallas_call x1, Pallas kernels, backward_pass(): pl.pallas_call(functools.partial(backward_kernel, n, ctx, tp, q_width, kv...  159 us
    pallas_call x1, Pallas kernels, forward_pass(): pl.pallas_call(functools.partial(forward_kernel, n, ctx, tp, q_width, kv_...  150 us

commit v1 on v0

--- a/solution.py
+++ b/solution.py
@@ -93,6 +93,19 @@
     low = lanes(v.shape) < HEAD_SIZE
     zero = jnp.zeros_like(v)
     return jnp.concatenate([jnp.where(low, v, zero), jnp.where(low, zero, v)], axis=0)
+
+
+def head_gains(gain_query, gain_key, q_width, kv_width, b):
+    key, value = q_width, q_width + kv_width
+    parts = [
+        gain_query[...]
+        if c < key
+        else gain_key[...]
+        if c < value
+        else jnp.ones((1, HEAD_SIZE), F32)
+        for c in (b, b + HEAD_SIZE)
+    ]
+    return jnp.concatenate(parts, axis=1)
 
 
 def one_row(v):
@@ -317,13 +330,13 @@
 
 def forward_kernel(
     n, ctx, tp, q_width, kv_width, tile,
-    lengths, tokens, cotangent, slots, gain, head_gain, gain_ffn, frequency,
+    lengths, tokens, cotangent, slots, gain, gain_query, gain_key, gain_ffn, frequency,
     w_query, w_key, w_value, w_out, w_gate, w_up, w_down,
     sums, squares, ffn_out, dmid, dgain, take_back, send_back, cosines, sines,
-    x, dy, qb_out, kv, heads_out, mid_own, w_attn, normed_two, hidden, d_gate, d_up,
-    sent_x, sent_y, got_x, got_y, own_x, own_y, x_land, y_land, pick, qb, heads, mid, nb,
-    w, w_ffn, kv_all, part, land, acc, total, bias, ffn_acc, dn_acc, acts,
-    route_send, route_recv, tp_send, tp_recv, kv_send, kv_recv, out_sem, act_sem, *gather_sems
+    x, dy, qb_out, kv, heads_out, mid_own, w_attn, normed_two, down_keep, d_gate, d_up,
+    sent_x, sent_y, got_x, got_y, own_x, own_y, x_land, y_land, pick, qb, heads, mid,
+    w, w_ffn, kv_all, part, land, bias, ffn_acc, dn_acc, acts, turned, d_keep, d_send, d_land,
+    route_send, route_recv, tp_send, tp_recv, kv_send, kv_recv, out_sem, act_sem, down_send, down_recv, *gather_sems
 ):
     place = Place(n, ctx, tp)
     group = n * ctx
@@ -461,7 +474,8 @@
             later = start_keys(place, kv_all, own_rows, kv_send, kv_recv)
         block = dot(normed, w[:, b : b + 128], 1, 0)
         is_value = lanes(block.shape) + b >= values_from
-        done = qk_forward(block, head_gain[:, b : b + 128], cosines[...], sines[...], is_value)
+        gains = head_gains(gain_query, gain_key, q_width, kv_width, b)
+        done = qk_forward(block, gains, cosines[...], sines[...], is_value)
         if b < q_width:
             qb[:, b : b + 128] = done.astype(BF)
         else:
@@ -487,11 +501,13 @@
                     part_sum = e[:, :128]
                     for b in range(128, piece, 128):
                         part_sum = part_sum + e[:, b : b + 128]
-                    acc[g, part, :] += dot(e.astype(BF), v2, 1, 0)
-                    total[g, part, :] += part_sum
+                    block = lane_block(2 * g + h)
+                    acc[:, block] += dot(e.astype(BF), v2, 1, 0)
+                    total[:, block] += part_sum
 
         over_key_heads(n_pairs, kv_width // HEAD_SIZE, heads_of)
 
+    acc, total = ffn_acc, dn_acc
     acc[...] = jnp.zeros_like(acc)
     total[...] = jnp.zeros_like(total)
     one_piece(place.c)
@@ -537,9 +553,13 @@
 
     ones = jnp.ones((8, 128), F32)
     for g in range(n_pairs):
-        row_total = jnp.sum(total[g], axis=1, keepdims=True)
-        heads[:, 128 * g : 128 * g + 128] = one_row(acc[g] / row_total)
-        sums[g] = 1.0 / dot(ones, total[g], 1, 1, lax.Precision.HIGHEST)
+        first_head, second_head = lane_block(2 * g), lane_block(2 * g + 1)
+        values, totals = (
+            jnp.concatenate([v[:, first_head], v[:, second_head]], axis=0) for v in (acc, total)
+        )
+        row_total = jnp.sum(totals, axis=1, keepdims=True)
+        heads[:, 128 * g : 128 * g + 128] = one_row(values / row_total)
+        sums[g] = 1.0 / dot(ones, totals, 1, 1, lax.Precision.HIGHEST)
     part[...] = dot(heads[...].astype(BF), w[:, q_width + 2 * kv_width :], 1, 1).astype(BF)
     attention = [
         remote(part, land.at[j - 1], tp_send.at[2, j], tp_recv.at[2, j], place.side(j))
@@ -580,6 +600,9 @@
     mid[...] = v + att
     store(mid.at[:, block_rows(place.t, feat)], mid_own)
     v = (v + att).astype(BF).astype(F32)
+    for copy in attention:
+        copy.wait_send()
+    nb = part
     nb[...] = (v * row_scale(v) * gain_ffn[...]).astype(BF)
     store(nb, normed_two)
     ffn_acc[...] = jnp.zeros_like(ffn_acc)
@@ -589,6 +612,7 @@
     for copy in wide_y:
         copy.wait_recv()
     store(y_land, dy)
+    turn_blocks(place, y_land, turned)
 
     def one_tile(i):
         at = lambda m: block_rows(3 * i + m, tile)
@@ -599,13 +623,35 @@
         sig = 1.0 / (1.0 + jnp.exp(-gate))
         silu = gate * sig
         out = block_rows(i, tile)
-        acts[0, :, out] = (silu * up).astype(BF)
-        acts[1, :, out] = (d_hidden * up * (sig * (1.0 + gate * (1.0 - sig)))).astype(BF)
-        acts[2, :, out] = (d_hidden * silu).astype(BF)
-        ffn_acc[...] += dot(acts[0, :, out], w_down, 1, 1)
-        dn_acc[...] += dot(acts[1, :, out], w_gate, 1, 1) + dot(acts[2, :, out], w_up, 1, 1)
+        hidden = (silu * up).astype(BF)
+        acts[0, :, out] = (d_hidden * up * (sig * (1.0 + gate * (1.0 - sig)))).astype(BF)
+        acts[1, :, out] = (d_hidden * silu).astype(BF)
+        ffn_acc[...] += dot(hidden, w_down, 1, 1)
+        dn_acc[...] += dot(acts[0, :, out], w_gate, 1, 1) + dot(acts[1, :, out], w_up, 1, 1)
+        d_keep[:, out] = dot(turned[: width // 2, :], hidden, 1, 0).astype(BF)
+        d_send[:, out] = dot(turned[width // 2 :, :], hidden, 1, 0).astype(BF)
 
     act_stores = []
+    sides_of = [pl.ds(cuts[i] * tile, (cuts[i + 1] - cuts[i]) * tile) for i in range(4)]
+    down_cores = [
+        remote(
+            d_send.at[:, cols],
+            d_land.at[:, cols],
+            down_send.at[i],
+            down_recv.at[i],
+            place.at(c=place.flip(1)),
+        )
+        for i, cols in enumerate(sides_of)
+    ]
+
+    def finish_down(i):
+        core_sum(d_keep.at[:, sides_of[i]], d_land.at[:, sides_of[i]], down_cores[i])
+        copy = pltpu.make_async_copy(
+            d_keep.at[:, sides_of[i]], down_keep.at[:, sides_of[i]], act_sem.at[2, i]
+        )
+        copy.start()
+        act_stores.append(copy)
+
     for i, g in enumerate(groups + [tail]):
         if i == 1:
             tail.advance(2)
@@ -619,8 +665,11 @@
             third.from_chip(3)
         g.finish()
         repeat(cuts[i + 1] - cuts[i], lambda k, i=i: one_tile(cuts[i] + k))
-        cols = pl.ds(cuts[i] * tile, (cuts[i + 1] - cuts[i]) * tile)
-        for m, out in enumerate((hidden, d_gate, d_up)):
+        down_cores[i].start()
+        if i:
+            finish_down(i - 1)
+        cols = sides_of[i]
+        for m, out in enumerate((d_gate, d_up)):
             copy = pltpu.make_async_copy(acts.at[m, :, cols], out.at[:, cols], act_sem.at[m, i])
             copy.start()
             act_stores.append(copy)
@@ -635,6 +684,7 @@
         ffn_out[r, :] = ffn_acc[r, :].astype(BF)
 
     repeat(rows // 128, finish_rows)
+    finish_down(3)
 
     @pl.when(core_bit == 0)
     def _():
@@ -649,10 +699,12 @@
         passed.wait_send()
 
     store(kv_all, kv)
-    for copy in route_x + route_y + wide_x + wide_y + attention:
+    for copy in route_x + route_y + wide_x + wide_y:
         copy.wait_send()
     for g in [attn, tail] + groups:
         g.drain()
+    for copy in down_cores:
+        copy.wait_send()
     for copy in stores + act_stores:
         copy.wait()
 
@@ -677,7 +729,7 @@
 
 
 def forward_pass(grid, q_width, kv_width, tile, *operands):
-    tokens, w_query, w_key, w_gate = operands[1], operands[8], operands[9], operands[12]
+    tokens, w_query, w_key, w_gate = operands[1], operands[9], operands[10], operands[13]
     rows, feat = tokens.shape
     n, ctx, tp = grid.n, grid.ctx, grid.tp
     width = feat * tp
@@ -691,7 +743,7 @@
     attn_width = 2 * w_query.shape[1] + 2 * w_key.shape[1]
     return pl.pallas_call(
         functools.partial(forward_kernel, n, ctx, tp, q_width, kv_width, tile),
-        in_specs=[pl.BlockSpec(memory_space=pltpu.SMEM)] + [vm] * 14,
+        in_specs=[pl.BlockSpec(memory_space=pltpu.SMEM)] + [vm] * 15,
         out_specs=[vm] * 9 + [ANYWHERE] * 11,
         out_shape=[
             shape((n_pairs, 8, 2 * rows), F32),
@@ -711,7 +763,7 @@
             shape((rows, feat), F32),
             shape((width, attn_width), BF),
             shape((rows, width), BF),
-            shape((rows, ff), BF),
+            shape((width // 2, ff), BF),
             shape((rows, ff), BF),
             shape((rows, ff), BF),
         ],
@@ -723,18 +775,19 @@
             V((rows, q_width), BF),
             V((rows, q_width), F32),
             V((rows, width), F32),
-            V((rows, width), BF),
             V((width, attn_width), BF),
             V((width, 3 * ff), BF),
             V((row_len, 2 * kv_width), BF),
             V((rows, width), BF),
             V((tp - 1, rows, width), BF),
-            V((n_pairs, 2 * rows, 128), F32),
-            V((n_pairs, 2 * rows, 128), F32),
             V((rows, rows), F32),
             V((rows, width), F32),
             V((rows, width), F32),
-            V((3, rows, ff), BF),
+            V((2, rows, ff), BF),
+            V((width, rows), BF),
+            V((width // 2, ff), BF),
+            V((width // 2, ff), BF),
+            V((width // 2, ff), BF),
             dma((2, group)),
             dma((2, group)),
             dma((3, tp)),
@@ -743,6 +796,8 @@
             dma((3,)),
             dma((8,)),
             dma((3, 4)),
+            dma((4,)),
+            dma((4,)),
             dma((6, n)),
             dma((6, n)),
             dma((5, n)),
@@ -868,8 +923,9 @@
 
         repeat(self.h // step, add)
 
-    def drain(self):
-        self.chip.wait_send()
+    def drain(self, chip=True):
+        if chip:
+            self.chip.wait_send()
         for ring, _, _ in self.rings:
             for copy in ring:
                 copy.wait_send()
@@ -882,15 +938,15 @@
 
 def backward_kernel(
     n, ctx, tp, q_width, kv_width, stage_cols,
-    lengths, ffn, dmid, sums, cosines, sines, pick_t, gain, head_gain,
-    gain_ffn_grad, squares, qb_in, kv_in, heads_in, w_in, dy_in, x_in, mid_in, normed_two, hidden, d_gate, d_up,
+    lengths, ffn, dmid, sums, cosines, sines, pick_t, gain, gain_query, gain_key,
+    gain_ffn_grad, squares, qb_in, kv_in, heads_in, w_in, dy_in, x_in, mid_in, normed_two, down_in, d_gate, d_up,
     back_o, back_g, sum_gate, sum_up, sum_down, sum_out, sum_qkv, small,
     qb, kv_all, heads, w, x, turned, stage, keep, send, core_land, chip_land, line_land,
     o_keep, o_send, o_core, o_chip, o_line, a_keep, a_send, a_core, a_chip, a_line,
     d_mid_own, d_attn, dob, delta, bias, dq_t, dkv, kv_land, tp_land, ffn_away, ffn_land, dx_away, dx_land,
     sent, small_mine, small_land, small_side,
     tp_send, tp_recv, route_send, route_recv, small_send, small_recv, kv_send, kv_recv, load_sem,
-    free_sem, *scatter_sems
+    *scatter_sems
 ):
     place = Place(n, ctx, tp)
     group = n * ctx
@@ -898,7 +954,7 @@
     feat = width // tp
     share = rows // group
     piece = rows
-    ff = hidden.shape[1]
+    ff = d_gate.shape[1]
     half = width // 2
     n_pairs = q_width // 128
     qkv_width = q_width + 2 * kv_width
@@ -918,7 +974,7 @@
     across_cores = [
         remote(src, dst, c_send.at[i], c_recv.at[i], place.at(c=place.flip(1)))
         for i, (src, dst) in enumerate(
-            [(send.at[m % 2], core_land.at[m % 2]) for m in range(3)]
+            [(send.at[m], core_land.at[m]) for m in range(2)]
             + [(o_send, o_core), (a_send, a_core)]
         )
     ]
@@ -959,8 +1015,8 @@
     for copy in dmid_sum:
         copy.start()
 
-    sources = (hidden, d_gate, d_up)
-    tiles = [(m, b) for m in range(3) for b in range(0, ff, stage_cols)]
+    sources = (d_gate, d_up)
+    tiles = [(m, b) for m in range(2) for b in range(0, ff, stage_cols)]
     loads = [
         pltpu.make_async_copy(
             sources[m].at[:, pl.ds(b, stage_cols)], stage.at[i % 2], load_sem.at[i]
@@ -972,49 +1028,40 @@
     load_dy = pltpu.make_async_copy(dy_in, dy, load_sem.at[len(tiles) + 1])
     load_x = pltpu.make_async_copy(x_in, x, load_sem.at[len(tiles) + 2])
     load_mid = pltpu.make_async_copy(mid_in, mid, load_sem.at[len(tiles) + 3])
-    load_dy.start()
+    load_down = pltpu.make_async_copy(down_in, keep.at[0], load_sem.at[len(tiles) + 4])
+    load_down.start()
+    load_n.start()
     loads[0].start()
-    load_n.start()
-    load_mid.start()
     more_loads = [
         pltpu.make_async_copy(src, dst, load_sem.at[len(tiles) + 5 + i])
         for i, (src, dst) in enumerate(((w_in, w), (qb_in, qb), (kv_in, kv_all), (heads_in, heads)))
     ]
-    for copy in more_loads:
+    for copy in [load_dy, load_mid] + more_loads:
         copy.start()
+    load_down.wait()
+    down.begin()
+    down_x.to_chip()
     fill_away(ffn_away, ffn)
-    load_dy.wait()
-    turn_blocks(place, dy, turned)
+    load_n.wait()
+    turn_blocks(place, d_attn, turned)
     sub = 256 if stage_cols % 256 == 0 else 128
     for i, (m, b) in enumerate(tiles):
         if i + 1 < len(tiles):
             loads[i + 1].start()
-        if b == 0 and m == 1:
-            load_n.wait()
-            turn_blocks(place, d_attn, turned)
         if m == 1 and b == ff // 2 // stage_cols * stage_cols:
-            core_sum(keep.at[0], core_land.at[0], across_cores[0])
-            down.begin()
-            down_x.to_chip()
-            pl.semaphore_signal(
-                free_sem, inc=1, device_id=place.at(c=place.flip(1)), device_id_type=MESH
-            )
-        if b == 0 and m == 2:
-            across_cores[0].wait_send()
-        if m == 2 and b == ff // 2 // stage_cols * stage_cols:
-            core_sum(keep.at[1], core_land.at[1], across_cores[1])
+            core_sum(keep.at[1], core_land.at[0], across_cores[0])
             gate.to_chip()
         loads[i].wait()
         for s in range(0, stage_cols, sub):
             right = stage[i % 2, :, s : s + sub]
             cols = slice(b + s, b + s + sub)
-            keep[m, :, cols] = dot(turned[:half, :], right, 1, 0).astype(BF)
-            send[m % 2, :, cols] = dot(turned[half:, :], right, 1, 0).astype(BF)
+            keep[m + 1, :, cols] = dot(turned[:half, :], right, 1, 0).astype(BF)
+            send[m, :, cols] = dot(turned[half:, :], right, 1, 0).astype(BF)
         if b + stage_cols == ff:
-            if m == 2:
-                pl.semaphore_wait(free_sem, 1)
             across_cores[m].start()
-    core_sum(keep.at[2], core_land.at[0], across_cores[2])
+    down.advance(1)
+    core_sum(keep.at[2], core_land.at[1], across_cores[1])
+    load_dy.wait()
 
     for copy in more_loads:
         copy.wait()
@@ -1081,7 +1128,7 @@
 
         over_key_heads(n_pairs, kv_width // HEAD_SIZE, heads_of)
 
-    down.advance(1)
+    down.advance(2)
     down_x.from_chip()
 
     sibling = place.at(c=place.flip(1))
@@ -1113,8 +1160,8 @@
     right = heads[...].astype(BF)
     o_keep[...] = dot(turned[:half, :], right, 1, 0).astype(BF)
     o_send[...] = dot(turned[half:, :], right, 1, 0).astype(BF)
-    across_cores[3].start()
-    down.advance(2)
+    across_cores[2].start()
+    down.advance(3)
     down_x.advance(1)
 
     @pl.when(x_bit == 1)
@@ -1125,12 +1172,8 @@
         to_chip.start()
 
     gate.from_chip()
-
-    @pl.when(x_bit == 0)
-    def _():
-        up.to_chip()
-
-    core_sum(o_keep, o_core, across_cores[3])
+    up.to_chip()
+    core_sum(o_keep, o_core, across_cores[2])
     out_sum.to_chip()
 
     @pl.when(core_bit == 1)
@@ -1168,15 +1211,7 @@
 
     repeat(rows // 128, own_gradient)
     load_x.start()
-
-    @pl.when(x_bit == 1)
-    def _():
-        to_chip.wait_send()
-        up.to_chip()
-
     one_piece(place.c)
-    down.advance(3)
-    down.to_chip()
     down_x.advance(2)
     gate.advance(1)
     normed = tp_land.at[0]
@@ -1211,7 +1246,12 @@
         raw = dot(normed[...], w[:, b : b + 128], 1, 0)
         is_value = lanes(grad.shape) + b >= values_from
         back, gain_grad = qk_backward(
-            grad, raw, head_gain[:, b : b + 128], cosines[...], sines[...], is_value
+            grad,
+            raw,
+            head_gains(gain_query, gain_key, q_width, kv_width, b),
+            cosines[...],
+            sines[...],
+            is_value,
         )
         small_mine[2:3, b : b + 128] = gain_grad
         d_qkv[:, b : b + 128] = back.astype(BF)
@@ -1233,7 +1273,7 @@
         cols = slice(b, b + 256)
         a_keep[:, cols] = dot(turned[:half, :], d_qkv[:, cols], 1, 0).astype(BF)
         a_send[:, cols] = dot(turned[half:, :], d_qkv[:, cols], 1, 0).astype(BF)
-    across_cores[4].start()
+    across_cores[3].start()
     down_x.advance(3)
     gate.advance(2)
     small_out = [
@@ -1245,10 +1285,7 @@
     for copy in small_out:
         copy.start()
     small_land[place.me] = small_mine[...]
-    core_sum(a_keep, a_core, across_cores[4])
-    qkv_sum.to_chip()
-    out_sum.from_chip()
-    up.from_chip()
+    core_sum(a_keep, a_core, across_cores[3])
 
     for copy in dx_sum:
         copy.wait_recv()
@@ -1267,18 +1304,23 @@
     for copy in route_g:
         copy.start()
     back_g[own, :] = dob[own, :]
+    up.chip.wait_send()
+    qkv_sum.to_chip()
+    down.to_chip()
     gate.advance(3)
+    out_sum.from_chip()
+    gate.finish(sum_gate)
+    up.from_chip()
     out_sum.advance(1)
     up.advance(1)
     qkv_sum.from_chip()
-    gate.finish(sum_gate)
     out_sum.advance(2)
     up.advance(2)
     qkv_sum.advance(1)
+    out_sum.advance(3)
     down.from_chip()
     down.finish(sum_down.at[:, pl.ds(0, cut)])
     down_x.finish(sum_down.at[:, pl.ds(cut, ff - cut)])
-    out_sum.advance(3)
     up.advance(3)
     qkv_sum.advance(2)
     out_sum.finish(sum_out)
@@ -1316,6 +1358,7 @@
     @pl.when(x_bit == 1)
     def _():
         to_passer.wait_send()
+        to_chip.wait_send()
 
     @pl.when(core_bit == 1)
     def _():
@@ -1323,16 +1366,17 @@
 
     for copy in dmid_sum + dx_sum + route_o + route_g + sides:
         copy.wait_send()
-    for copy in across_cores[1:]:
+    for copy in across_cores:
         copy.wait_send()
-    for s in (down, down_x, gate, up, out_sum, qkv_sum):
+    for s in (down, down_x, gate, out_sum, qkv_sum):
         s.drain()
+    up.drain(chip=False)
 
 
 def backward_pass(grid, q_width, kv_width, *operands):
-    dmid, hidden = operands[2], operands[19]
+    dmid, d_gate = operands[2], operands[21]
     rows, width = dmid.shape
-    ff = hidden.shape[1]
+    ff = d_gate.shape[1]
     n, ctx, tp = grid.n, grid.ctx, grid.tp
     group = n * ctx
     feat = width // tp
@@ -1356,7 +1400,7 @@
 
     return pl.pallas_call(
         functools.partial(backward_kernel, n, ctx, tp, q_width, kv_width, stage_cols),
-        in_specs=[pl.BlockSpec(memory_space=pltpu.SMEM)] + [vm] * 10 + [ANYWHERE] * 11,
+        in_specs=[pl.BlockSpec(memory_space=pltpu.SMEM)] + [vm] * 11 + [ANYWHERE] * 11,
         out_specs=[vm] * 8,
         out_shape=[
             shape((rows, feat), BF),
@@ -1410,10 +1454,9 @@
             dma((2, max(group, tp))),
             dma((3,)),
             dma((3,)),
-            dma((3 * (ff // stage_cols) + 9,)),
-            pltpu.SemaphoreType.REGULAR,
-            dma((5,)),
-            dma((5,)),
+            dma((2 * (ff // stage_cols) + 9,)),
+            dma((4,)),
+            dma((4,)),
             dma((7,)),
             dma((7,)),
             dma((7, n)),
@@ -1507,18 +1550,11 @@
     kv_width = key_value_heads * HEAD_SIZE
     ff = w_gate.shape[1]
     tile = 256 if ff % 256 == 0 else 128
-    head_gain = jnp.concatenate(
-        [
-            jnp.tile(gain_query, q_heads),
-            jnp.tile(gain_key, key_value_heads),
-            jnp.ones((kv_width,), F32),
-        ]
-    )[None, :]
     frequency = ROPE_THETA ** (-np.arange(0, HEAD_SIZE, 2, dtype=np.float64) / HEAD_SIZE)
     frequency = jnp.asarray(np.tile(frequency, 4)[None, :], F32)
     (
         sums, squares, ffn_part, d_mid_part, d_gain_ffn, take_back, send_back, cosines, sines,
-        x_full, dy_full, qb, row_kv, heads, middle_own, attn_w, normed_two, hidden, d_gate, d_up,
+        x_full, dy_full, qb, row_kv, heads, middle_own, attn_w, normed_two, down_keep, d_gate, d_up,
     ) = forward_pass(
         grid,
         q_width,
@@ -1529,7 +1565,8 @@
         cotangent,
         slot_of.reshape(-1, 128),
         gain_attn[None, :],
-        head_gain,
+        gain_query[None, :],
+        gain_key[None, :],
         gain_ffn[None, :],
         frequency,
         w_query,
@@ -1552,7 +1589,8 @@
         sines,
         take_back,
         gain_attn[None, :],
-        head_gain,
+        gain_query[None, :],
+        gain_key[None, :],
         d_gain_ffn,
         squares,
         qb,
@@ -1563,7 +1601,7 @@
         x_full,
         middle_own,
         normed_two,
-        hidden,
+        down_keep,
         d_gate,
         d_up,
     )

time: 321 us -> 313 us (0.975)
  Pallas kernels: 313 us -> 307 us
    pallas_call x1, Pallas kernels: 159 us -> 150 us  [backward_pass(): pl.pallas_call(functools.partial(backward_kernel, n, ctx, tp, q_width, kv...]
where the time goes in v1:
time: 313 us; the launch traced here: 309 us
  Pallas kernels  307 us (98%)
    pallas_call x1, Pallas kernels, forward_pass(): pl.pallas_call(functools.partial(forward_kernel, n, ctx, tp, q_width, kv_...  152 us
    pallas_call x1, Pallas kernels, backward_pass(): pl.pallas_call(functools.partial(backward_kernel, n, ctx, tp, q_width, kv...  150 us

profile of v1, /device:TPU:0, one launch (start us, length us, event | category | flops | bytes accessed | tf_op | source)
XLA Modules:
  0.0 309.1 jit_solution(8549124751803022793)
XLA Ops:
  0.6 152.4 %shard_map.263 = (f32[4,8,1024]{2,1,0:T(8,128)}, f32[2,1024]{1,0:T(2,128)}, bf16[512,1024]{1,0:T(8,128)(2,1)}, bf16[512,1024]{1,0:T(8,128)(2,1)}, f32[1,1024]{1,...) custom-call(s32[1,3]{1,0:T(1,128)} %lengths.3, ...), custom_call_target="tpu_custom_call" | custom-call | flops 14495514624 | bytes 41943040 | tf_op jit(solution)/shard_map/pallas_call | solution.py:744
  153.0 150.4 %shard_map.264 = (bf16[512,512]{1,0:T(8,128)(2,1)}, bf16[512,512]{1,0:T(8,128)(2,1)}, f32[64,2304]{1,0:T(8,128)}, f32[64,2304]{1,0:T(8,128)}, f32[64,2304]{1,0:T...) custom-call(s32[1,3]{1,0:T(1,128)} %lengths.3, bf16[512,1024]{1,0:T(8,128)(2,1)} %get-tuple-element.56.ffn, ...), custom_call_target="tpu_custom_call" | custom-call | flops 10737418240 | bytes 41943040 | tf_op jit(solution)/shard_map/pallas_call | solution.py:1401
  303.4 4.3 %shard_map.265 = (bf16[512,512]{1,0:T(8,128)(2,1)}, bf16[512,512]{1,0:T(8,128)(2,1)}, f32[64,512]{1,0:T(8,128)}, f32[64,256]{1,0:T(8,128)}, f32[64,256]{1,0:T(8,...) custom-call(bf16[512,512]{1,0:T(8,128)(2,1)} %get-tuple-element.75.p, ...), custom_call_target="tpu_custom_call" | custom-call | tf_op jit(solution)/shard_map/pallas_call | solution.py:1519
  307.8 1.1 slice_bitcast_fusion

commit v2 on v1

--- a/solution.py
+++ b/solution.py
@@ -964,11 +964,13 @@
     c_send, c_recv, *ring_sems = scatter_sems
     everything = pl.ds(0, ff)
     lands = lambda m: (chip_land.at[m], line_land.at[m])
-    cut = ff // 128 * 11 // 18 * 128
+    cut = ff // 128 * 16 // 18 * 128
     down = Scatter(place, keep.at[0], pl.ds(0, cut), *lands(0), 0, ring_sems, True)
     down_x = Scatter(place, keep.at[0], pl.ds(cut, ff - cut), *lands(0), 6, ring_sems)
     gate = Scatter(place, keep.at[1], everything, *lands(1), 2, ring_sems)
-    up = Scatter(place, keep.at[2], everything, *lands(2), 3, ring_sems)
+    mid_cut = ff // 256 * 128
+    up_a = Scatter(place, keep.at[2], pl.ds(0, mid_cut), *lands(2), 3, ring_sems)
+    up_b = Scatter(place, keep.at[2], pl.ds(mid_cut, ff - mid_cut), *lands(2), 7, ring_sems)
     out_sum = Scatter(place, o_keep, pl.ds(0, q_width), o_chip, o_line, 4, ring_sems)
     qkv_sum = Scatter(place, a_keep, pl.ds(0, qkv_width), a_chip, a_line, 5, ring_sems)
     across_cores = [
@@ -1172,7 +1174,7 @@
         to_chip.start()
 
     gate.from_chip()
-    up.to_chip()
+    up_a.to_chip()
     core_sum(o_keep, o_core, across_cores[2])
     out_sum.to_chip()
 
@@ -1212,6 +1214,7 @@
     repeat(rows // 128, own_gradient)
     load_x.start()
     one_piece(place.c)
+    up_b.to_chip()
     down_x.advance(2)
     gate.advance(1)
     normed = tp_land.at[0]
@@ -1286,6 +1289,7 @@
         copy.start()
     small_land[place.me] = small_mine[...]
     core_sum(a_keep, a_core, across_cores[3])
+    up_a.from_chip()
 
     for copy in dx_sum:
         copy.wait_recv()
@@ -1304,27 +1308,31 @@
     for copy in route_g:
         copy.start()
     back_g[own, :] = dob[own, :]
-    up.chip.wait_send()
+    up_a.advance(1)
+    up_b.chip.wait_send()
     qkv_sum.to_chip()
     down.to_chip()
     gate.advance(3)
     out_sum.from_chip()
+    up_a.advance(2)
     gate.finish(sum_gate)
-    up.from_chip()
+    up_b.from_chip()
     out_sum.advance(1)
-    up.advance(1)
+    up_a.advance(3)
+    up_b.advance(1)
     qkv_sum.from_chip()
     out_sum.advance(2)
-    up.advance(2)
+    up_b.advance(2)
     qkv_sum.advance(1)
     out_sum.advance(3)
     down.from_chip()
     down.finish(sum_down.at[:, pl.ds(0, cut)])
     down_x.finish(sum_down.at[:, pl.ds(cut, ff - cut)])
-    up.advance(3)
+    up_a.finish(sum_up.at[:, pl.ds(0, mid_cut)])
+    up_b.advance(3)
     qkv_sum.advance(2)
     out_sum.finish(sum_out)
-    up.finish(sum_up)
+    up_b.finish(sum_up.at[:, pl.ds(mid_cut, ff - mid_cut)])
     for copy in small_out:
         copy.wait_recv()
     total = small_land[0]
@@ -1368,9 +1376,9 @@
         copy.wait_send()
     for copy in across_cores:
         copy.wait_send()
-    for s in (down, down_x, gate, out_sum, qkv_sum):
+    for s in (down, down_x, gate, up_a, out_sum, qkv_sum):
         s.drain()
-    up.drain(chip=False)
+    up_b.drain(chip=False)
 
 
 def backward_pass(grid, q_width, kv_width, *operands):
@@ -1457,10 +1465,10 @@
             dma((2 * (ff // stage_cols) + 9,)),
             dma((4,)),
             dma((4,)),
-            dma((7,)),
-            dma((7,)),
-            dma((7, n)),
-            dma((7, n)),
+            dma((8,)),
+            dma((8,)),
+            dma((8, n)),
+            dma((8, n)),
         ],
         compiler_params=pltpu.CompilerParams(
             vmem_limit_bytes=61 * 2**20, collective_id=1, has_side_effects=True

time: 313 us -> 312 us (level)
  no operation moved by 1% of the time
where the time goes in v2:
time: 312 us; the launch traced here: 309 us
  Pallas kernels  307 us (98%)
    pallas_call x1, Pallas kernels, forward_pass(): pl.pallas_call(functools.partial(forward_kernel, n, ctx, tp, q_width, kv_...  152 us
    pallas_call x1, Pallas kernels, backward_pass(): pl.pallas_call(functools.partial(backward_kernel, n, ctx, tp, q_width, kv...  150 us

profile of v2, /device:TPU:0, one launch (start us, length us, event | category | flops | bytes accessed | tf_op | source)
XLA Modules:
  0.0 308.7 jit_solution(6875375223545266906)
XLA Ops:
  0.6 152.4 %shard_map.263 = (f32[4,8,1024]{2,1,0:T(8,128)}, f32[2,1024]{1,0:T(2,128)}, bf16[512,1024]{1,0:T(8,128)(2,1)}, bf16[512,1024]{1,0:T(8,128)(2,1)}, f32[1,1024]{1,...) custom-call(s32[1,3]{1,0:T(1,128)} %lengths.3, ...), custom_call_target="tpu_custom_call" | custom-call | flops 14495514624 | bytes 41943040 | tf_op jit(solution)/shard_map/pallas_call | solution.py:744
  153.0 150.0 %shard_map.264 = (bf16[512,512]{1,0:T(8,128)(2,1)}, bf16[512,512]{1,0:T(8,128)(2,1)}, f32[64,2304]{1,0:T(8,128)}, f32[64,2304]{1,0:T(8,128)}, f32[64,2304]{1,0:T...) custom-call(s32[1,3]{1,0:T(1,128)} %lengths.3, bf16[512,1024]{1,0:T(8,128)(2,1)} %get-tuple-element.56.ffn, ...), custom_call_target="tpu_custom_call" | custom-call | flops 10737418240 | bytes 41943040 | tf_op jit(solution)/shard_map/pallas_call | solution.py:1409
  303.1 4.3 %shard_map.265 = (bf16[512,512]{1,0:T(8,128)(2,1)}, bf16[512,512]{1,0:T(8,128)(2,1)}, f32[64,512]{1,0:T(8,128)}, f32[64,256]{1,0:T(8,128)}, f32[64,256]{1,0:T(8,...) custom-call(bf16[512,512]{1,0:T(8,128)(2,1)} %get-tuple-element.75.p, ...), custom_call_target="tpu_custom_call" | custom-call | tf_op jit(solution)/shard_map/pallas_call | solution.py:1527
  307.4 1.1 slice_bitcast_fusion
